TPU v7x, 32 devices: a whole 2x2x4 slice. The times are simulated.
32 devices in a mesh: dp: 2 (over x), fsdp: 16 (over z, y, core).
Axes of the slice: x: 2, y: 2, z: 4, core: 2. Of those that a mesh axis runs over, the one named last changes fastest.
Arguments:
- tokens: bfloat16 [4096, 3584], P(('dp', 'fsdp')), may hold values from -6 to 6
- out_grad: bfloat16 [4096, 14336], P(('dp', 'fsdp')), may hold values from -6 to 6
- block_values: bfloat16 [80, 128, 128], P('fsdp'), may hold values from -0.625 to 0.625
- active_blocks: int32 [80, 2], P('fsdp'), may hold values from 0 to 111
- drop_slots: int32 [16], P('fsdp'), may hold values from 0 to 4, as said below
- cand_blocks: int32 [16, 2], replicated, may hold values from 0 to 111, as said below
- group_counts: int32 [2], P('dp'), may hold values from 1024 to 2048
Outputs:
- cand_grad: float32 [16, 128, 128], P('fsdp')
- cand_score: float32 [16], P('fsdp')
Inputs may be any that keep to these rules, and one draw needn't show every extreme that they name: `drop_slots`: the 1 entries of each device are distinct local slots. `cand_blocks`: pairs of block row and block column, distinct, none of them a stored block.
All inputs are finite; a program needn't handle non-finite values.
Results may differ from a plain program's by a relative error of at most 0.007.
Values may be sent and summed in bfloat16 or wider, within the bound.
A program may use at most 128 MiB of HBM per device.

v0:
```python
import jax
import jax.numpy as jnp
from jax import lax
from jax.sharding import PartitionSpec as P


def gelu_slope(value_in):
    normal_cdf = 0.5 * (1.0 + jax.scipy.special.erf(value_in * 0.7071067811865476))
    density = jnp.exp(-0.5 * value_in * value_in) * 0.3989422804014327
    return normal_cdf + value_in * density


def per_device(
    tokens, out_grad, block_values, active_blocks, drop_slots, cand_blocks, group_counts
):
    rows_dev = tokens.shape[0]
    block_size = block_values.shape[1]
    row_blocks = tokens.shape[1] // block_size
    hidden = out_grad.shape[1]
    col_blocks = hidden // block_size
    local_blocks = block_values.shape[0]
    cand_total = cand_blocks.shape[0]
    tok_blocks = tokens.reshape(rows_dev, row_blocks, block_size)
    slot_ids = jnp.arange(local_blocks, dtype=jnp.int32)
    dropped = jnp.any(slot_ids[:, None] == drop_slots[None, :], axis=1)
    kept_flag = 1 - dropped.astype(jnp.int32)
    empty = jnp.zeros((rows_dev, col_blocks, block_size), jnp.float32)
    masked = block_values * kept_flag.astype(jnp.bfloat16)[:, None, None]
    weights = lax.all_gather(masked, "fsdp", axis=0, tiled=True)
    places = lax.all_gather(active_blocks, "fsdp", axis=0, tiled=True)
    picked = tok_blocks[:, places[:, 0], :]
    product = jnp.einsum("tkb,kbc->tkc", picked, weights, preferred_element_type=jnp.float32)
    preact = empty.at[:, places[:, 1], :].add(product)
    position = lax.axis_index("fsdp") * rows_dev + jnp.arange(rows_dev, dtype=jnp.int32)
    usable = (position < group_counts[0]).astype(jnp.float32)
    cand_x = tok_blocks[:, cand_blocks[:, 0], :]
    preact = preact.reshape(rows_dev, hidden)
    pre_grad = (out_grad.astype(jnp.float32) * gelu_slope(preact) * usable[:, None]).astype(
        jnp.bfloat16
    )
    cand_dy = pre_grad.reshape(rows_dev, col_blocks, block_size)[:, cand_blocks[:, 1], :]
    cand_local = cand_total // lax.axis_size("fsdp")
    term = jnp.einsum("tcb,tce->cbe", cand_x, cand_dy, preferred_element_type=jnp.float32)
    shared = lax.psum_scatter(
        term.reshape(cand_local * block_size * lax.axis_size("fsdp"), block_size),
        "fsdp",
        scatter_dimension=0,
        tiled=True,
    )
    summed = lax.psum(shared, "dp")
    scale = (rows_dev * lax.axis_size("dp") * lax.axis_size("fsdp")) ** (-0.5)
    cand_grad = summed.reshape(cand_local, block_size, block_size) * scale
    cand_score = jnp.sqrt(jnp.mean(cand_grad * cand_grad, axis=(1, 2)) + 1e-06)
    return (cand_grad, cand_score)


def solution(mesh):
    return jax.shard_map(
        per_device,
        mesh=mesh,
        in_specs=(
            P(("dp", "fsdp"), None),
            P(("dp", "fsdp"), None),
            P("fsdp", None, None),
            P("fsdp", None),
            P("fsdp"),
            P(),
            P("dp"),
        ),
        out_specs=(P("fsdp", None, None), P("fsdp")),
        check_vma=False,
    )
```

profile of v0, /device:TPU:0, one launch (start us, length us, event | category | flops | bytes accessed | tf_op | source)
XLA Modules:
  0.0 198.0 jit_solution(15918346221816714215)
XLA Ops:
  7.2 0.0 all-gather.3.cloned.1.call-start
  7.9 1.7 broadcast_multiply_fusion
  9.5 0.0 all-gather.3.cloned.1.call-update
  9.5 0.0 reduce-scatter.2.cloned.1.call-start
  9.6 1.6 copy.24
  11.2 0.0 copy-start.1
  11.2 0.6 copy.25
  11.8 23.4 %all-gather = s32[16,5,2]{1,2,0:T(2,128)S(1)} all-gather(s32[1,5,2]{1,2,0:T(2,128)} %bitcast.45), channel_id=1, replica_groups=mesh['dp'=2,'fsdp'=16] {'fsdp'}, dimensions={0}, use_global_device_ids=true | all-gather | bytes 680 | tf_op jit(solution)/shard_map/all_gather | solution.py:30
  35.2 0.1 reshape.82
  35.3 5.9 %copy.26 = bf16[128,14336]{0,1:T(8,128)(2,1)} copy(bf16[128,14336]{1,0:T(8,128)(2,1)} %param.8) | data formatting | bytes 7340032 | tf_op args[1]
  41.8 1.1 gather_fusion.1
  42.9 0.0 copy-done.1
  42.9 1.4 gather_fusion
  44.3 11.9 %all-gather.3.cloned.1.call-done = bf16[80,128,128]{2,1,0:T(8,128)(2,1)} async-done(((bf16[5,128,128]{2,1,0:T(8,128)(2,1)}), bf16[80,128,128]{2,1,0:T(8,128)(2,1)}) %all-gather.3.cloned.1.call-update) | async-done | bytes 2621456 | tf_op jit(solution)/shard_map/all_gather | solution.py:29
  56.3 4.9 %fusion.10 = f32[80,128,128]{2,1,0:T(8,128)} fusion(bf16[80,128,128]{2,1,0:T(8,128)(2,1)} %all-gather.3.cloned.1.call-done, bf16[80,128,128]{2,1,0:T(8,128)(2,1)S(1)} %gather_fusion.1), kind=kOutput, calls=%fused_computation.16 | convolution fusion | flops 335544320 | bytes 10485760 | tf_op jit(solution)/shard_map/tkb,kbc->tkc/dot_general | solution.py:32
  61.1 3.9 %broadcast_in_dim.2 = f32[128,112,128]{2,0,1:T(8,128)} broadcast(f32[]{:T(128)} %constant.17.clone.1), dimensions={} | broadcast | bytes 7340036 | tf_op jit(solution)/shard_map/broadcast_in_dim | solution.py:27
  65.1 17.0 %scatter_fusion = f32[128,112,128]{2,0,1:T(8,128)} fusion(f32[128,112,128]{2,0,1:T(8,128)} %broadcast_in_dim.2, s32[80]{0:T(128)S(1)} %get-tuple-element.7, f32[80,128,128]{2,1,0:T(8,128)} %fusion.10), kind=kCustom, calls=%fused_computation.3 | custom fusion | flops 1310720 | bytes 15728960 | tf_op jit(solution)/shard_map/scatter-add | solution.py:33
  82.0 8.6 %copy.29 = f32[128,112,128]{0,2,1:T(8,128)} copy(f32[128,112,128]{2,0,1:T(8,128)} %scatter_fusion) | data formatting | bytes 14680064 | tf_op jit(solution)/shard_map/scatter-add | solution.py:33
  90.7 8.4 %fusion.6 = bf16[128,14336]{0,1:T(8,128)(2,1)} fusion(f32[128,112,128]{0,2,1:T(8,128)} %copy.29, bf16[128,14336]{0,1:T(8,128)(2,1)} %copy.26, f32[128]{0:T(128)S(1)} %compare_convert_fusion), kind=kLoop, calls=%fused_computation.11 | loop fusion | flops 22020096 | bytes 14680576 | tf_op jit(solution)/shard_map/convert_element_type | solution.py:38
  99.0 0.0 copy-start
  99.0 6.1 %copy.30 = bf16[128,112,128]{2,0,1:T(8,128)(2,1)} copy(bf16[128,112,128]{0,2,1:T(8,128)(2,1)} %bitcast.42) | data formatting | bytes 7340032 | tf_op jit(solution)/shard_map/reshape | solution.py:41
  105.2 2.7 %gather_fusion.2 = bf16[16,128,128]{2,1,0:T(8,128)(2,1)S(1)} fusion(bf16[128,112,128]{2,0,1:T(8,128)(2,1)} %copy.30, s32[1024]{0:T(1024)S(1)} %get-tuple-element.8), kind=kCustom, calls=%fused_computation.2 | custom fusion | bytes 1048640 | tf_op jit(solution)/shard_map/gather | solution.py:41
  107.9 0.0 copy-done
  107.9 1.3 fusion.12
  109.2 0.0 reduce-scatter.2.cloned.1.call-update
  109.2 0.0 all-reduce.2.cloned.1.call-start
  109.3 56.2 %reduce-scatter.2.cloned.1.call-done = f32[128,128]{1,0:T(8,128)} async-done(((f32[2048,128]{1,0:T(8,128)}), f32[128,128]{1,0:T(8,128)}) %reduce-scatter.2.cloned.1.call-update) | async-done | bytes 65552 | tf_op jit(solution)/shard_map/reduce_scatter | solution.py:44
  165.5 0.0 all-reduce.2.cloned.1.call-update
  165.5 22.1 %all-reduce.2.cloned.1.call-done = f32[128,128]{1,0:T(8,128)} async-done(((f32[128,128]{1,0:T(8,128)}), f32[128,128]{1,0:T(8,128)}) %all-reduce.2.cloned.1.call-update) | async-done | bytes 65552 | tf_op jit(solution)/shard_map/psum | solution.py:50
  187.6 2.1 %multiply_reduce_fusion = (f32[]{:T(128)}, f32[1,128,128]{2,1,0:T(8,128)}) fusion(f32[128,128]{1,0:T(8,128)} %all-reduce.2.cloned.1.call-done), kind=kLoop, calls=%fused_computation.22 | loop fusion | flops 49151 | bytes 131076 | tf_op jit(solution)/shard_map/reduce_sum | solution.py:53
  (7 shorter events, 0.0 us)
Async XLA Ops:
  7.2 49.1 %all-gather.3.cloned.1.call-start = ((), (), s32[]{:S(2)}) async-start(), calls=%async_computation.1 | async-start | bytes 2785280 | tf_op jit(solution)/shard_map/all_gather | solution.py:29
  9.5 155.9 %reduce-scatter.2.cloned.1.call-start = ((), (), s32[]{:S(2)}) async-start(), calls=%async_computation.2 | async-start | bytes 1114112 | tf_op jit(solution)/shard_map/reduce_scatter | solution.py:44
  11.2 31.7 %copy-start.1 = (s32[16,2]{0,1:T(2,128)S(1)}, s32[16,2]{0,1:T(2,128)}, u32[]{:S(2)}) copy-start(s32[16,2]{0,1:T(2,128)} %param.12) | copy-start | bytes 388
  99.0 8.8 %copy-start = (bf16[16,128,128]{2,1,0:T(8,128)(2,1)S(1)}, bf16[16,128,128]{2,1,0:T(8,128)(2,1)}, u32[]{:S(2)}) copy-start(bf16[16,128,128]{2,1,0:T(8,128)(2,1)} %gather_fusion) | copy-start | bytes 1572868
  109.2 78.4 %all-reduce.2.cloned.1.call-start = ((), (), s32[]{:S(2)}) async-start(), calls=%async_computation.3 | async-start | bytes 131072 | tf_op jit(solution)/shard_map/psum | solution.py:50
Sparse Core Ops, SparseCore 0:
  10.3 45.9 all-gather.2
  109.4 56.0 reduce-scatter.1
  167.8 19.7 all-reduce.1
where the time goes:
time: 199 us; the launch traced here: 198 us
  waiting for transfers between devices  90.2 us (45%)
  local copies, waits for them, and re-layouts  32 us (16%)
  other arithmetic  29.1 us (15%)
  blocking collectives  23.4 us (12%)
  between operations  17 us (9%)
  matrix products  6.19 us (3%)
    reduce_scatter x1, waiting for transfers between devices, per_device(): lax.psum_scatter(term.reshape(cand_local * block_size * lax.axis_size('fs...  56.2 us
    all_gather x1, blocking collectives, per_device(): places = lax.all_gather(active_blocks, 'fsdp', axis=0, tiled=True)  23.4 us
    psum x1, waiting for transfers between devices, per_device(): summed = lax.psum(shared, 'dp')  22.1 us
    scatter-add x1, other arithmetic, per_device(): preact = empty.at[:, places[:, 1], :].add(product)  17 us
    all_gather x1, waiting for transfers between devices, per_device(): weights = lax.all_gather(masked, 'fsdp', axis=0, tiled=True)  11.9 us
    scatter-add x1, local copies, waits for them, and re-layouts, per_device(): preact = empty.at[:, places[:, 1], :].add(product)  8.64 us
    convert_element_type x1, other arithmetic, per_device(): (out_grad.astype(jnp.float32) * gelu_slope(preact) * usable[:, None]).ast...  8.38 us
    unnamed x7, local copies, waits for them, and re-layouts  7.55 us
  transfers between devices with their start and end apart: 3, of which 3 were waited for; matrix products, arithmetic and copies ran while one was open for 5% of the time, Pallas kernels for 0%

commit v1 on v0

v1 whole, which is shorter than its diff:
```python
import functools
import jax
import jax.numpy as jnp
from jax import lax
from jax.experimental import pallas as pl
from jax.experimental.pallas import tpu as pltpu
from jax.sharding import PartitionSpec as P

MESH = pl.DeviceIdType.MESH


def gelu_slope(value_in):
    normal_cdf = 0.5 * (1.0 + lax.erf(value_in * 0.7071067811865476))
    density = jnp.exp(-0.5 * value_in * value_in) * 0.3989422804014327
    return normal_cdf + value_in * density


def kernel(
    dims,
    tok_hbm, og_hbm, bv_hbm, active, drops, cands, counts,
    grad_out, score_out,
    tok, og, bv, gath, meta_v, meta_s, xt, prod, acc,
    send_a, recv_a, own_a, send_c, recv_c, own_c, send_d, recv_d, share_b,
    load_sem, meta_send, meta_recv, meta_load, chunk_send, chunk_recv,
    a_send, a_recv, c_send, c_recv, d_send, d_recv, b_send, b_recv,
):
    n_dp, n_f, outer, inner = dims
    blk = bv.shape[1]
    stored = bv.shape[0]
    kept = stored - 1
    n_cand = acc.shape[0]
    dp = lax.axis_index("dp")
    me = lax.axis_index("fsdp")
    core = me % 2
    my_b = (me // 2) % inner
    my_a = me // (2 * inner)
    sibling = me + 1 - 2 * core

    def index(a, b, c):
        return (a * inner + b) * 2 + c

    load_bv = pltpu.make_async_copy(bv_hbm, bv, load_sem.at[0])
    load_bv.start()

    def load_columns(hbm, held, sem):
        @pl.loop(0, held.shape[0])
        def _(at):
            column = pl.multiple_of(at * blk, blk)
            pltpu.make_async_copy(hbm.at[:, pl.ds(column, blk)], held.at[at], sem).start()

    def wait_columns(held, sem):
        pltpu.make_async_copy(held, held, sem).wait()

    barrier = pltpu.get_barrier_semaphore()

    @pl.loop(1, n_f)
    def _(step):
        pl.semaphore_signal(
            barrier, inc=1, device_id={"fsdp": (me + step) % n_f}, device_id_type=MESH
        )

    @pl.loop(1, n_dp)
    def _(step):
        pl.semaphore_signal(
            barrier, inc=1, device_id={"dp": (dp + step) % n_dp}, device_id_type=MESH
        )

    load_columns(tok_hbm, tok, load_sem.at[1])
    drop = drops[0]
    lane = lax.broadcasted_iota(jnp.int32, (1, 128), 1)
    places = jnp.zeros((1, 128), jnp.int32)
    load_bv.wait()
    for slot in range(kept):
        at = slot + jnp.where(drop <= slot, 1, 0)
        gath[me, slot * blk:(slot + 1) * blk, :] = bv[at]
        places = jnp.where(lane == 2 * slot, active[at, 0], places)
        places = jnp.where(lane == 2 * slot + 1, active[at, 1], places)
    meta_v[me] = places

    pl.semaphore_wait(barrier, n_f - 1 + n_dp - 1)

    def chunk_copy(source, way, target):
        return pltpu.make_async_remote_copy(
            src_ref=gath.at[source],
            dst_ref=gath.at[source],
            send_sem=chunk_send.at[way, source],
            recv_sem=chunk_recv.at[source],
            device_id={"fsdp": target},
            device_id_type=MESH,
        )

    def meta_copy(step):
        target = (me + step) % n_f
        return pltpu.make_async_remote_copy(
            src_ref=meta_v.at[me],
            dst_ref=meta_v.at[me],
            send_sem=meta_send.at[step],
            recv_sem=meta_recv.at[me],
            device_id={"fsdp": target},
            device_id_type=MESH,
        )

    def meta_arrival(source):
        return pltpu.make_async_remote_copy(
            src_ref=meta_v.at[source],
            dst_ref=meta_v.at[source],
            send_sem=meta_send.at[0],
            recv_sem=meta_recv.at[source],
            device_id={"fsdp": sibling},
            device_id_type=MESH,
        )

    def forwards(a, b, act):
        source = index(a, b, core)

        @pl.when((b == my_b) & (a >= my_a) & (my_a > 0))
        def _():
            act(chunk_copy(source, 0, index(my_a - 1, my_b, core)))

        @pl.when((b == my_b) & (a <= my_a) & (my_a < outer - 1))
        def _():
            act(chunk_copy(source, 1, index(my_a + 1, my_b, core)))

        @pl.when((b >= my_b) & (my_b > 0))
        def _():
            act(chunk_copy(source, 2, index(my_a, my_b - 1, core)))

        @pl.when((b <= my_b) & (my_b < inner - 1))
        def _():
            act(chunk_copy(source, 3, index(my_a, my_b + 1, core)))

        act(chunk_copy(source, 4, sibling))

    def around(step, mine):
        return mine + (1 - 2 * (step % 2)) * ((step + 1) // 2)

    forwards(my_a, my_b, lambda copy: copy.start())

    @pl.loop(1, n_f)
    def _(step):
        meta_copy(step).start()

    load_columns(og_hbm, og, load_sem.at[2])
    wait_columns(tok, load_sem.at[1])

    @pl.loop(0, n_cand)
    def _(c):
        xt[c] = tok[cands[c, 0]].T
        acc[c] = jnp.zeros((blk, blk), jnp.float32)

    @pl.loop(1, n_f)
    def _(step):
        meta_arrival((me + step) % n_f).wait_recv()

    to_scalars = pltpu.make_async_copy(meta_v, meta_s, meta_load)
    to_scalars.start()
    to_scalars.wait()

    def process(source):
        for slot in range(kept):
            prod[slot] = jnp.dot(
                tok[meta_s[source, 0, 2 * slot]],
                gath[source, slot * blk:(slot + 1) * blk, :],
                preferred_element_type=jnp.float32,
            )
        columns = [meta_s[source, 0, 2 * slot + 1] for slot in range(kept)]

        @pl.loop(0, n_cand)
        def _(c):
            column = cands[c, 1]
            total = acc[c]
            for slot in range(kept):
                total = total + jnp.where(columns[slot] == column, 1.0, 0.0) * prod[slot]
            acc[c] = total

    @pl.loop(0, 2 * outer - 1)
    def _(i):
        a = around(i, my_a)

        @pl.loop(0, 2 * inner - 1)
        def _(j):
            b = around(j, my_b)

            @pl.when((a >= 0) & (a < outer) & (b >= 0) & (b < inner))
            def _():
                source = index(a, b, core)

                @pl.when(i + j > 0)
                def _():
                    chunk_copy(source, 4, sibling).wait_recv()
                    forwards(a, b, lambda copy: copy.start())

                process(source)
                other = index(a, b, 1 - core)
                chunk_copy(other, 4, sibling).wait_recv()
                process(other)

    wait_columns(og, load_sem.at[2])
    position = me * blk + lax.broadcasted_iota(jnp.int32, (blk, 1), 0)
    usable = jnp.where(position < counts[0], 1.0, 0.0)

    def term(c):
        slope = gelu_slope(acc[c])
        pre_grad = og[cands[c, 1]].astype(jnp.float32) * slope * usable
        return jnp.dot(xt[c], pre_grad.astype(jnp.bfloat16), preferred_element_type=jnp.float32)

    def a_copy(a, b):
        at = a * inner + b
        return pltpu.make_async_remote_copy(
            src_ref=send_a.at[at], dst_ref=recv_a.at[at],
            send_sem=a_send.at[at], recv_sem=a_recv.at[at],
            device_id={"fsdp": sibling}, device_id_type=MESH,
        )

    def c_copy(a, step):
        return pltpu.make_async_remote_copy(
            src_ref=send_c.at[step, a], dst_ref=recv_c.at[step, a],
            send_sem=c_send.at[step, a], recv_sem=c_recv.at[step, a],
            device_id={"fsdp": index(my_a, (my_b + step) % inner, core)}, device_id_type=MESH,
        )

    def d_copy(step):
        return pltpu.make_async_remote_copy(
            src_ref=send_d.at[step], dst_ref=recv_d.at[step],
            send_sem=d_send.at[step], recv_sem=d_recv.at[step],
            device_id={"fsdp": index((my_a + step) % outer, my_b, core)}, device_id_type=MESH,
        )

    def b_copy(step):
        return pltpu.make_async_remote_copy(
            src_ref=share_b.at[0], dst_ref=share_b.at[step],
            send_sem=b_send.at[step], recv_sem=b_recv.at[step],
            device_id={"dp": (dp + step) % n_dp}, device_id_type=MESH,
        )

    def every(act):
        @pl.loop(1, inner + 1)
        def _(step):
            b = (my_b + step) % inner

            @pl.loop(1, outer + 1)
            def _(hop):
                act(step, b, (my_a + hop) % outer)

    def for_sibling(step, b, a):
        send_a[a * inner + b] = term(index(a, b, 1 - core)).astype(jnp.bfloat16)
        a_copy(a, b).start()

    every(for_sibling)

    def for_mine(step, b, a):
        own_a[...] = term(index(a, b, core))
        a_copy(a, b).wait_recv()
        total = own_a[...] + recv_a[a * inner + b].astype(jnp.float32)

        @pl.when(step < inner)
        def _():
            send_c[step, a] = total.astype(jnp.bfloat16)
            c_copy(a, step).start()

        @pl.when(step == inner)
        def _():
            own_c[a] = total

    every(for_mine)

    @pl.loop(1, outer + 1)
    def _(hop):
        a = (my_a + hop) % outer
        total = own_c[a]
        for step in range(1, inner):
            c_copy(a, step).wait_recv()
            total = total + recv_c[step, a].astype(jnp.float32)

        @pl.when(hop < outer)
        def _():
            send_d[hop] = total.astype(jnp.bfloat16)
            d_copy(hop).start()

        @pl.when(hop == outer)
        def _():
            own_c[a] = total

    total = own_c[my_a]
    for hop in range(1, outer):
        d_copy(hop).wait_recv()
        total = total + recv_d[hop].astype(jnp.float32)
    share_b[0] = total.astype(jnp.bfloat16)
    for step in range(1, n_dp):
        b_copy(step).start()
    for step in range(1, n_dp):
        b_copy(step).wait_recv()
    total = jnp.zeros((blk, blk), jnp.float32)
    for group in range(n_dp):
        total = total + share_b[(dp - group + n_dp) % n_dp].astype(jnp.float32)
    scale = (blk * n_dp * n_f) ** (-0.5)
    total = total * scale
    grad_out[0] = total
    score = jnp.sqrt(jnp.sum(total * total, keepdims=True) * (1.0 / (blk * blk)) + 1e-06)
    score_out[0] = score[0, 0]

    @pl.loop(1, n_f)
    def _(step):
        meta_copy(step).wait_send()

    @pl.loop(0, outer)
    def _(a):
        @pl.loop(0, inner)
        def _(b):
            forwards(a, b, lambda copy: copy.wait_send())
            a_copy(a, b).wait_send()

        for step in range(1, inner):
            c_copy(a, step).wait_send()

    for hop in range(1, outer):
        d_copy(hop).wait_send()
    for step in range(1, n_dp):
        b_copy(step).wait_send()


def per_device(
    n_dp, n_f,
    tokens, out_grad, block_values, active_blocks, drop_slots, cand_blocks, group_counts
):
    rows, _ = tokens.shape
    stored, blk, _ = block_values.shape
    n_cand = cand_blocks.shape[0]
    outer = 4
    inner = n_f // (2 * outer)
    kept = stored - 1
    bf16, f32, i32 = jnp.bfloat16, jnp.float32, jnp.int32
    half = n_cand // 2
    sem = pltpu.SemaphoreType.DMA
    return pl.pallas_call(
        functools.partial(kernel, (n_dp, n_f, outer, inner)),
        out_shape=(
            jax.ShapeDtypeStruct((1, blk, blk), f32),
            jax.ShapeDtypeStruct((1,), f32),
        ),
        in_specs=[pl.BlockSpec(memory_space=pl.ANY)] * 3
        + [pl.BlockSpec(memory_space=pltpu.SMEM)] * 4,
        out_specs=(
            pl.BlockSpec(memory_space=pltpu.VMEM),
            pl.BlockSpec(memory_space=pltpu.SMEM),
        ),
        scratch_shapes=[
            pltpu.VMEM((tokens.shape[1] // blk, rows, blk), bf16),
            pltpu.VMEM((out_grad.shape[1] // blk, rows, blk), bf16),
            pltpu.VMEM(block_values.shape, bf16),
            pltpu.VMEM((n_f, kept * blk, blk), bf16),
            pltpu.VMEM((n_f, 1, 128), i32),
            pltpu.SMEM((n_f, 1, 128), i32),
            pltpu.VMEM((n_cand, blk, rows), bf16),
            pltpu.VMEM((kept, rows, blk), f32),
            pltpu.VMEM((n_cand, rows, blk), f32),
            pltpu.VMEM((half, blk, blk), bf16),
            pltpu.VMEM((half, blk, blk), bf16),
            pltpu.VMEM((blk, blk), f32),
            pltpu.VMEM((inner, outer, blk, blk), bf16),
            pltpu.VMEM((inner, outer, blk, blk), bf16),
            pltpu.VMEM((outer, blk, blk), f32),
            pltpu.VMEM((outer, blk, blk), bf16),
            pltpu.VMEM((outer, blk, blk), bf16),
            pltpu.VMEM((n_dp, blk, blk), bf16),
            sem((3,)), sem((n_f,)), sem((n_f,)), sem(()), sem((5, n_f)), sem((n_f,)),
            sem((half,)), sem((half,)), sem((inner, outer)), sem((inner, outer)),
            sem((outer,)), sem((outer,)), sem((n_dp,)), sem((n_dp,)),
        ],
        compiler_params=pltpu.CompilerParams(
            collective_id=0, has_side_effects=True, vmem_limit_bytes=48 * 1024 * 1024
        ),
        cost_estimate=pl.CostEstimate(
            flops=2 * blk ** 3 * (n_f * kept + n_cand),
            bytes_accessed=2 * (tokens.size + out_grad.size),
            transcendentals=n_cand * blk * blk,
        ),
    )(tokens, out_grad, block_values, active_blocks, drop_slots, cand_blocks, group_counts)


def solution(mesh):
    return jax.shard_map(
        functools.partial(per_device, mesh.shape["dp"], mesh.shape["fsdp"]),
        mesh=mesh,
        in_specs=(
            P(("dp", "fsdp"), None),
            P(("dp", "fsdp"), None),
            P("fsdp", None, None),
            P("fsdp", None),
            P("fsdp"),
            P(),
            P("dp"),
        ),
        out_specs=(P("fsdp", None, None), P("fsdp")),
        check_vma=False,
    )
```

time: 199 us -> 66.1 us (0.33)
  waiting for transfers between devices: 90.2 us -> 0 us
  Pallas kernels: 0 us -> 55.9 us
  other arithmetic: 29.1 us -> 0 us
  local copies, waits for them, and re-layouts: 32 us -> 6.28 us
  blocking collectives: 23.4 us -> 0 us
  between operations: 17 us -> 3.67 us
  matrix products: 6.19 us -> 0 us
    reduce_scatter x1 -> x0, waiting for transfers between devices: 56.2 us -> none  [per_device(): lax.psum_scatter(term.reshape(cand_local * block_size * lax.axis_size('fs...]
    pallas_call x0 -> x1, Pallas kernels: none -> 55.9 us  [per_device(): pl.pallas_call(functools.partial(kernel, (n_dp, n_f, outer, inner)), out_...]
    all_gather x1 -> x0, blocking collectives: 23.4 us -> none  [per_device(): places = lax.all_gather(active_blocks, 'fsdp', axis=0, tiled=True)]
    psum x1 -> x0, waiting for transfers between devices: 22.1 us -> none  [per_device(): summed = lax.psum(shared, 'dp')]
    scatter-add x1 -> x0, other arithmetic: 17 us -> none  [per_device(): preact = empty.at[:, places[:, 1], :].add(product)]
    all_gather x1 -> x0, waiting for transfers between devices: 11.9 us -> none  [per_device(): weights = lax.all_gather(masked, 'fsdp', axis=0, tiled=True)]
    scatter-add x1 -> x0, local copies, waits for them, and re-layouts: 8.64 us -> none  [per_device(): preact = empty.at[:, places[:, 1], :].add(product)]
    convert_element_type x3 -> x0, other arithmetic: 8.39 us -> none  [the longest x1 8.38 us: per_device(): (out_grad.astype(jnp.float32) * gelu_slope(preact) * usable[:, None]).ast...]
  transfers between devices with their start and end apart: 3 -> 0, of which waited for: 3 -> 0; matrix products, arithmetic and copies ran while one was open for 5% -> 0% of each run, Pallas kernels for 0% -> 0%
where the time goes in v1:
time: 66.1 us; the launch traced here: 65.9 us
  Pallas kernels  55.9 us (85%)
  local copies, waits for them, and re-layouts  6.28 us (10%)
  between operations  3.67 us (6%)
    pallas_call x1, Pallas kernels, per_device(): pl.pallas_call(functools.partial(kernel, (n_dp, n_f, outer, inner)), out_...  55.9 us
    unnamed x9, local copies, waits for them, and re-layouts  6.28 us

profile of v1, /device:TPU:0, one launch (start us, length us, event | category | flops | bytes accessed | tf_op | source)
XLA Modules:
  0.0 65.9 jit_solution(4306173792340773714)
XLA Ops:
  1.9 0.8 %copy.9.active = s32[5,2]{1,0:T(8,128)S(1)} copy(s32[5,2]{0,1:T(2,128)} %param.10) | data formatting | bytes 80 | tf_op args[3]
  2.7 0.8 %copy.10.cands = s32[16,2]{1,0:T(8,128)S(1)} copy(s32[16,2]{0,1:T(2,128)} %param.12) | data formatting | bytes 256 | tf_op args[5]
  3.4 0.0 copy-start
  3.4 2.0 %copy-done = bf16[128,14336]{1,0:T(8,128)(2,1)S(1)} copy-done((bf16[128,14336]{1,0:T(8,128)(2,1)S(1)}, bf16[128,14336]{1,0:T(8,128)(2,1)}, u32[]{:S(2)}) %copy-start) | copy-done | bytes 3670040
  5.5 0.0 copy-start.1
  5.5 1.2 %copy-done.1 = bf16[128,3584]{1,0:T(8,128)(2,1)S(1)} copy-done((bf16[128,3584]{1,0:T(8,128)(2,1)S(1)}, bf16[128,3584]{1,0:T(8,128)(2,1)}, u32[]{:S(2)}) %copy-start.1) | copy-done | bytes 917528
  6.7 0.0 copy-start.2
  6.7 0.9 %copy-done.2 = bf16[5,128,128]{2,1,0:T(8,128)(2,1)S(1)} copy-done((bf16[5,128,128]{2,1,0:T(8,128)(2,1)S(1)}, bf16[5,128,128]{2,1,0:T(8,128)(2,1)}, u32[]{:S(2)}) %copy-start.2) | copy-done | bytes 163864
  7.6 55.9 %shard_map.86 = (f32[1,128,128]{2,1,0:T(8,128)S(1)}, f32[1]{0:T(128)}) custom-call(bf16[128,3584]{1,0:T(8,128)(2,1)S(1)} %copy-done.1, bf16[128,14336]{1,0:T(8,128)(2,1)S(1)} %copy-done, bf16[5,128,128]{2,1,0:T(8,128)(2,1)S(1)} %copy-done.2, s32[5,2]{1,0:T(8,128)S(1)} %copy.9.active, s32[1]{0:T(128)S(6)} %copy.13.drops, s32[16,2]{1,0:T(8,128)S(1)} %copy.10.cands, ...), custom_call_target="tpu_custom_call" | custom-call | flops 335544320 | bytes 4587520 | tf_op jit(solution)/shard_map/pallas_call | solution.py:335
  63.5 0.6 copy.15
Async XLA Ops:
  3.4 2.0 %copy-start = (bf16[128,14336]{1,0:T(8,128)(2,1)S(1)}, bf16[128,14336]{1,0:T(8,128)(2,1)}, u32[]{:S(2)}) copy-start(bf16[128,14336]{1,0:T(8,128)(2,1)} %og_hbm.1) | copy-start | bytes 11010052
  5.5 1.2 %copy-start.1 = (bf16[128,3584]{1,0:T(8,128)(2,1)S(1)}, bf16[128,3584]{1,0:T(8,128)(2,1)}, u32[]{:S(2)}) copy-start(bf16[128,3584]{1,0:T(8,128)(2,1)} %tok_hbm.1) | copy-start | bytes 2752516
  6.7 0.9 %copy-start.2 = (bf16[5,128,128]{2,1,0:T(8,128)(2,1)S(1)}, bf16[5,128,128]{2,1,0:T(8,128)(2,1)}, u32[]{:S(2)}) copy-start(bf16[5,128,128]{2,1,0:T(8,128)(2,1)} %bv_hbm.1) | copy-start | bytes 491524

commit v2 on v1

--- a/solution.py
+++ b/solution.py
@@ -73,8 +73,8 @@
     for slot in range(kept):
         at = slot + jnp.where(drop <= slot, 1, 0)
         gath[me, slot * blk:(slot + 1) * blk, :] = bv[at]
-        places = jnp.where(lane == 2 * slot, active[at, 0], places)
-        places = jnp.where(lane == 2 * slot + 1, active[at, 1], places)
+        places = jnp.where(lane == 2 * slot, active[0, at], places)
+        places = jnp.where(lane == 2 * slot + 1, active[1, at], places)
     meta_v[me] = places
 
     pl.semaphore_wait(barrier, n_f - 1 + n_dp - 1)
@@ -134,19 +134,14 @@
     def around(step, mine):
         return mine + (1 - 2 * (step % 2)) * ((step + 1) // 2)
 
-    forwards(my_a, my_b, lambda copy: copy.start())
-
     @pl.loop(1, n_f)
     def _(step):
         meta_copy(step).start()
 
+    forwards(my_a, my_b, lambda copy: copy.start())
     load_columns(og_hbm, og, load_sem.at[2])
     wait_columns(tok, load_sem.at[1])
-
-    @pl.loop(0, n_cand)
-    def _(c):
-        xt[c] = tok[cands[c, 0]].T
-        acc[c] = jnp.zeros((blk, blk), jnp.float32)
+    acc[...] = jnp.zeros(acc.shape, jnp.float32)
 
     @pl.loop(1, n_f)
     def _(step):
@@ -164,14 +159,21 @@
                 preferred_element_type=jnp.float32,
             )
         columns = [meta_s[source, 0, 2 * slot + 1] for slot in range(kept)]
-
-        @pl.loop(0, n_cand)
-        def _(c):
-            column = cands[c, 1]
-            total = acc[c]
-            for slot in range(kept):
-                total = total + jnp.where(columns[slot] == column, 1.0, 0.0) * prod[slot]
-            acc[c] = total
+        for top in range(0, blk, 64):
+            part = [prod[slot, top:top + 64, :] for slot in range(kept)]
+
+            @pl.loop(0, n_cand // 16)
+            def _(group):
+                for at in range(16):
+                    c = group * 16 + at
+                    column = cands[1, c]
+                    total = acc[c, top:top + 64, :]
+                    for slot in range(kept):
+                        chosen = jnp.where(columns[slot] == column, 1.0, 0.0)
+                        total = total + chosen * part[slot]
+                    acc[c, top:top + 64, :] = total
+
+    turned = n_cand // (outer * inner)
 
     @pl.loop(0, 2 * outer - 1)
     def _(i):
@@ -183,17 +185,24 @@
 
             @pl.when((a >= 0) & (a < outer) & (b >= 0) & (b < inner))
             def _():
-                source = index(a, b, core)
-
                 @pl.when(i + j > 0)
                 def _():
-                    chunk_copy(source, 4, sibling).wait_recv()
+                    chunk_copy(index(a, b, core), 4, sibling).wait_recv()
                     forwards(a, b, lambda copy: copy.start())
 
-                process(source)
-                other = index(a, b, 1 - core)
-                chunk_copy(other, 4, sibling).wait_recv()
-                process(other)
+                for at in range(turned):
+                    c = (a * inner + b) * turned + at
+                    xt[c] = tok[cands[0, c]].T
+
+                @pl.loop(0, 2)
+                def _(turn):
+                    source = index(a, b, (core + turn) % 2)
+
+                    @pl.when(turn == 1)
+                    def _():
+                        chunk_copy(source, 4, sibling).wait_recv()
+
+                    process(source)
 
     wait_columns(og, load_sem.at[2])
     position = me * blk + lax.broadcasted_iota(jnp.int32, (blk, 1), 0)
@@ -201,7 +210,7 @@
 
     def term(c):
         slope = gelu_slope(acc[c])
-        pre_grad = og[cands[c, 1]].astype(jnp.float32) * slope * usable
+        pre_grad = og[cands[1, c]].astype(jnp.float32) * slope * usable
         return jnp.dot(xt[c], pre_grad.astype(jnp.bfloat16), preferred_element_type=jnp.float32)
 
     def a_copy(a, b):
@@ -238,29 +247,34 @@
         def _(step):
             b = (my_b + step) % inner
 
-            @pl.loop(1, outer + 1)
-            def _(hop):
-                act(step, b, (my_a + hop) % outer)
-
-    def for_sibling(step, b, a):
-        send_a[a * inner + b] = term(index(a, b, 1 - core)).astype(jnp.bfloat16)
-        a_copy(a, b).start()
+            @pl.loop(0, outer // 2)
+            def _(pair):
+                act(step, b, [(my_a + 2 * pair + hop) % outer for hop in (1, 2)])
+
+    def for_sibling(step, b, pair):
+        found = [term(index(a, b, 1 - core)) for a in pair]
+        for a, value in zip(pair, found):
+            send_a[a * inner + b] = value.astype(jnp.bfloat16)
+            a_copy(a, b).start()
 
     every(for_sibling)
 
-    def for_mine(step, b, a):
-        own_a[...] = term(index(a, b, core))
-        a_copy(a, b).wait_recv()
-        total = own_a[...] + recv_a[a * inner + b].astype(jnp.float32)
-
-        @pl.when(step < inner)
-        def _():
-            send_c[step, a] = total.astype(jnp.bfloat16)
-            c_copy(a, step).start()
-
-        @pl.when(step == inner)
-        def _():
-            own_c[a] = total
+    def for_mine(step, b, pair):
+        found = [term(index(a, b, core)) for a in pair]
+        for at, value in enumerate(found):
+            own_a[at] = value
+        for at, a in enumerate(pair):
+            a_copy(a, b).wait_recv()
+            total = own_a[at] + recv_a[a * inner + b].astype(jnp.float32)
+
+            @pl.when(step < inner)
+            def _():
+                send_c[step, a] = total.astype(jnp.bfloat16)
+                c_copy(a, step).start()
+
+            @pl.when(step == inner)
+            def _():
+                own_c[a] = total
 
     every(for_mine)
 
@@ -356,7 +370,7 @@
             pltpu.VMEM((n_cand, rows, blk), f32),
             pltpu.VMEM((half, blk, blk), bf16),
             pltpu.VMEM((half, blk, blk), bf16),
-            pltpu.VMEM((blk, blk), f32),
+            pltpu.VMEM((2, blk, blk), f32),
             pltpu.VMEM((inner, outer, blk, blk), bf16),
             pltpu.VMEM((inner, outer, blk, blk), bf16),
             pltpu.VMEM((outer, blk, blk), f32),
@@ -368,14 +382,16 @@
             sem((outer,)), sem((outer,)), sem((n_dp,)), sem((n_dp,)),
         ],
         compiler_params=pltpu.CompilerParams(
-            collective_id=0, has_side_effects=True, vmem_limit_bytes=48 * 1024 * 1024
+            collective_id=0, has_side_effects=True, vmem_limit_bytes=64 * 1024 * 1024
         ),
         cost_estimate=pl.CostEstimate(
             flops=2 * blk ** 3 * (n_f * kept + n_cand),
             bytes_accessed=2 * (tokens.size + out_grad.size),
             transcendentals=n_cand * blk * blk,
         ),
-    )(tokens, out_grad, block_values, active_blocks, drop_slots, cand_blocks, group_counts)
+    )(
+        tokens, out_grad, block_values, active_blocks.T, drop_slots, cand_blocks.T, group_counts
+    )
 
 
 def solution(mesh):

time: 66.1 us -> 57.8 us (0.87)
  local copies, waits for them, and re-layouts: 6.28 us -> 1.47 us
  Pallas kernels: 55.9 us -> 52.4 us
    unnamed x9 -> x1, local copies, waits for them, and re-layouts: 6.28 us -> 1.47 us
    pallas_call x1, Pallas kernels: 55.9 us -> 52.4 us  [per_device(): pl.pallas_call(functools.partial(kernel, (n_dp, n_f, outer, inner)), out_...]
where the time goes in v2:
time: 57.8 us; the launch traced here: 57.5 us
  Pallas kernels  52.4 us (91%)
  between operations  3.68 us (6%)
  local copies, waits for them, and re-layouts  1.47 us (3%)
    pallas_call x1, Pallas kernels, per_device(): pl.pallas_call(functools.partial(kernel, (n_dp, n_f, outer, inner)), out_...  52.4 us
    unnamed x1, local copies, waits for them, and re-layouts  1.47 us

profile of v2, /device:TPU:0, one launch (start us, length us, event | category | flops | bytes accessed | tf_op | source)
XLA Modules:
  0.0 57.5 jit_solution(4511158339342793192)
XLA Ops:
  1.9 52.4 %shard_map.86 = (f32[1,128,128]{2,1,0:T(8,128)}, f32[1]{0:T(128)}) custom-call(bf16[128,3584]{1,0:T(8,128)(2,1)} %tok_hbm.1, bf16[128,14336]{1,0:T(8,128)(2,1)} %og_hbm.1, bf16[5,128,128]{2,1,0:T(8,128)(2,1)} %bv_hbm.1, s32[2,5]{1,0:T(2,128)} %bitcast.2, s32[1]{0:T(128)S(6)} %copy.11.drops, s32[2,16]{1,0:T(2,128)} %bitcast.3, s32[1]{0:T(128)S(6)} %copy.12.counts), custom_call_target="tpu_custom_call" | custom-call | flops 335544320 | bytes 4587520 | tf_op jit(solution)/shard_map/pallas_call | solution.py:349
  54.3 1.5 %copy.13 = f32[1,128,128]{2,1,0:T(8,128)} copy(f32[1,128,128]{2,1,0:T(8,128)} %get-tuple-element.4) | data formatting | bytes 131072

commit v3 on v2

--- a/solution.py
+++ b/solution.py
@@ -28,6 +28,7 @@
     blk = bv.shape[1]
     stored = bv.shape[0]
     kept = stored - 1
+    half_slots = kept // 2
     n_cand = acc.shape[0]
     dp = lax.axis_index("dp")
     me = lax.axis_index("fsdp")
@@ -42,11 +43,17 @@
     load_bv = pltpu.make_async_copy(bv_hbm, bv, load_sem.at[0])
     load_bv.start()
 
-    def load_columns(hbm, held, sem):
-        @pl.loop(0, held.shape[0])
-        def _(at):
-            column = pl.multiple_of(at * blk, blk)
-            pltpu.make_async_copy(hbm.at[:, pl.ds(column, blk)], held.at[at], sem).start()
+    def load_columns(hbm, held, sem, part, parts):
+        share = pl.cdiv(held.shape[0], parts)
+
+        @pl.loop(0, share)
+        def _(step):
+            at = part * share + step
+
+            @pl.when(at < held.shape[0])
+            def _():
+                column = pl.multiple_of(at * blk, blk)
+                pltpu.make_async_copy(hbm.at[:, pl.ds(column, blk)], held.at[at], sem).start()
 
     def wait_columns(held, sem):
         pltpu.make_async_copy(held, held, sem).wait()
@@ -65,27 +72,41 @@
             barrier, inc=1, device_id={"dp": (dp + step) % n_dp}, device_id_type=MESH
         )
 
-    load_columns(tok_hbm, tok, load_sem.at[1])
+    load_columns(tok_hbm, tok, load_sem.at[1], 0, 1)
     drop = drops[0]
     lane = lax.broadcasted_iota(jnp.int32, (1, 128), 1)
     places = jnp.zeros((1, 128), jnp.int32)
     load_bv.wait()
     for slot in range(kept):
         at = slot + jnp.where(drop <= slot, 1, 0)
-        gath[me, slot * blk:(slot + 1) * blk, :] = bv[at]
+        held, place = slot // half_slots, slot % half_slots
+        gath[me, held, place * blk:(place + 1) * blk, :] = bv[at]
         places = jnp.where(lane == 2 * slot, active[0, at], places)
         places = jnp.where(lane == 2 * slot + 1, active[1, at], places)
     meta_v[me] = places
 
     pl.semaphore_wait(barrier, n_f - 1 + n_dp - 1)
 
+    mine = dp % 2
+    partner = dp + 1 - 2 * mine
+
     def chunk_copy(source, way, target):
         return pltpu.make_async_remote_copy(
             src_ref=gath.at[source],
             dst_ref=gath.at[source],
             send_sem=chunk_send.at[way, source],
-            recv_sem=chunk_recv.at[source],
+            recv_sem=chunk_recv.at[2, source],
             device_id={"fsdp": target},
+            device_id_type=MESH,
+        )
+
+    def half_copy(source, half, way, device):
+        return pltpu.make_async_remote_copy(
+            src_ref=gath.at[source, half],
+            dst_ref=gath.at[source, half],
+            send_sem=chunk_send.at[way, source],
+            recv_sem=chunk_recv.at[half, source],
+            device_id=device,
             device_id_type=MESH,
         )
 
@@ -110,36 +131,47 @@
             device_id_type=MESH,
         )
 
-    def forwards(a, b, act):
+    def along_outer(a, act):
+        source = index(a, my_b, core)
+
+        @pl.when((a >= my_a) & (my_a > 0))
+        def _():
+            act(chunk_copy(source, 0, index(my_a - 1, my_b, core)))
+
+        @pl.when((a <= my_a) & (my_a < outer - 1))
+        def _():
+            act(chunk_copy(source, 1, index(my_a + 1, my_b, core)))
+
+        act(chunk_copy(source, 4, sibling))
+
+    def along_inner(a, b, act):
         source = index(a, b, core)
 
-        @pl.when((b == my_b) & (a >= my_a) & (my_a > 0))
-        def _():
-            act(chunk_copy(source, 0, index(my_a - 1, my_b, core)))
-
-        @pl.when((b == my_b) & (a <= my_a) & (my_a < outer - 1))
-        def _():
-            act(chunk_copy(source, 1, index(my_a + 1, my_b, core)))
-
         @pl.when((b >= my_b) & (my_b > 0))
         def _():
-            act(chunk_copy(source, 2, index(my_a, my_b - 1, core)))
+            act(half_copy(source, mine, 2, {"fsdp": index(my_a, my_b - 1, core)}))
 
         @pl.when((b <= my_b) & (my_b < inner - 1))
         def _():
-            act(chunk_copy(source, 3, index(my_a, my_b + 1, core)))
-
-        act(chunk_copy(source, 4, sibling))
-
-    def around(step, mine):
-        return mine + (1 - 2 * (step % 2)) * ((step + 1) // 2)
+            act(half_copy(source, mine, 3, {"fsdp": index(my_a, my_b + 1, core)}))
+
+    def across(a, b, act):
+        source = index(a, b, core)
+        act(half_copy(source, mine, 5, {"dp": partner}))
+        act(half_copy(source, mine, 4, {"fsdp": sibling}))
+
+    def last_half(a, b):
+        return half_copy(index(a, b, core), 1 - mine, 6, {"fsdp": sibling})
+
+    def around(step, centre):
+        return centre + (1 - 2 * (step % 2)) * ((step + 1) // 2)
 
     @pl.loop(1, n_f)
     def _(step):
         meta_copy(step).start()
 
-    forwards(my_a, my_b, lambda copy: copy.start())
-    load_columns(og_hbm, og, load_sem.at[2])
+    along_inner(my_a, my_b, lambda copy: copy.start())
+    along_outer(my_a, lambda copy: copy.start())
     wait_columns(tok, load_sem.at[1])
     acc[...] = jnp.zeros(acc.shape, jnp.float32)
 
@@ -155,7 +187,7 @@
         for slot in range(kept):
             prod[slot] = jnp.dot(
                 tok[meta_s[source, 0, 2 * slot]],
-                gath[source, slot * blk:(slot + 1) * blk, :],
+                gath[source, slot // half_slots, pl.ds(slot % half_slots * blk, blk), :],
                 preferred_element_type=jnp.float32,
             )
         columns = [meta_s[source, 0, 2 * slot + 1] for slot in range(kept)]
@@ -185,10 +217,24 @@
 
             @pl.when((a >= 0) & (a < outer) & (b >= 0) & (b < inner))
             def _():
-                @pl.when(i + j > 0)
+                source = index(a, b, core)
+                other = index(a, b, 1 - core)
+
+                @pl.when((j == 0) & (i > 0))
                 def _():
-                    chunk_copy(index(a, b, core), 4, sibling).wait_recv()
-                    forwards(a, b, lambda copy: copy.start())
+                    chunk_copy(source, 4, sibling).wait_recv()
+                    along_outer(a, lambda copy: copy.start())
+                    along_inner(a, b, lambda copy: copy.start())
+
+                @pl.when(j > 0)
+                def _():
+                    half_copy(source, mine, 4, {"fsdp": sibling}).wait_recv()
+                    across(a, b, lambda copy: copy.start())
+                    along_inner(a, b, lambda copy: copy.start())
+                    last_half(a, b).wait_recv()
+                    last_half(a, b).start()
+
+                load_columns(og_hbm, og, load_sem.at[2], a * inner + b, outer * inner)
 
                 for at in range(turned):
                     c = (a * inner + b) * turned + at
@@ -198,9 +244,14 @@
                 def _(turn):
                     source = index(a, b, (core + turn) % 2)
 
-                    @pl.when(turn == 1)
+                    @pl.when((turn == 1) & (j == 0))
                     def _():
-                        chunk_copy(source, 4, sibling).wait_recv()
+                        chunk_copy(other, 4, sibling).wait_recv()
+
+                    @pl.when((turn == 1) & (j > 0))
+                    def _():
+                        half_copy(other, 0, 4, {"fsdp": sibling}).wait_recv()
+                        half_copy(other, 1, 4, {"fsdp": sibling}).wait_recv()
 
                     process(source)
 
@@ -321,8 +372,17 @@
     def _(a):
         @pl.loop(0, inner)
         def _(b):
-            forwards(a, b, lambda copy: copy.wait_send())
+            along_inner(a, b, lambda copy: copy.wait_send())
             a_copy(a, b).wait_send()
+
+            @pl.when(b == my_b)
+            def _():
+                along_outer(a, lambda copy: copy.wait_send())
+
+            @pl.when(b != my_b)
+            def _():
+                across(a, b, lambda copy: copy.wait_send())
+                last_half(a, b).wait_send()
 
         for step in range(1, inner):
             c_copy(a, step).wait_send()
@@ -362,7 +422,7 @@
             pltpu.VMEM((tokens.shape[1] // blk, rows, blk), bf16),
             pltpu.VMEM((out_grad.shape[1] // blk, rows, blk), bf16),
             pltpu.VMEM(block_values.shape, bf16),
-            pltpu.VMEM((n_f, kept * blk, blk), bf16),
+            pltpu.VMEM((n_f, 2, kept // 2 * blk, blk), bf16),
             pltpu.VMEM((n_f, 1, 128), i32),
             pltpu.SMEM((n_f, 1, 128), i32),
             pltpu.VMEM((n_cand, blk, rows), bf16),
@@ -377,7 +437,7 @@
             pltpu.VMEM((outer, blk, blk), bf16),
             pltpu.VMEM((outer, blk, blk), bf16),
             pltpu.VMEM((n_dp, blk, blk), bf16),
-            sem((3,)), sem((n_f,)), sem((n_f,)), sem(()), sem((5, n_f)), sem((n_f,)),
+            sem((3,)), sem((n_f,)), sem((n_f,)), sem(()), sem((7, n_f)), sem((3, n_f)),
             sem((half,)), sem((half,)), sem((inner, outer)), sem((inner, outer)),
             sem((outer,)), sem((outer,)), sem((n_dp,)), sem((n_dp,)),
         ],

time: 57.8 us -> 67.2 us (1.16)
  Pallas kernels: 52.4 us -> 61.9 us
    pallas_call x1, Pallas kernels: 52.4 us -> 61.9 us  [per_device(): pl.pallas_call(functools.partial(kernel, (n_dp, n_f, outer, inner)), out_...]
where the time goes in v3:
time: 67.2 us; the launch traced here: 67 us
  Pallas kernels  61.9 us (92%)
  between operations  3.68 us (5%)
  local copies, waits for them, and re-layouts  1.47 us (2%)
    pallas_call x1, Pallas kernels, per_device(): pl.pallas_call(functools.partial(kernel, (n_dp, n_f, outer, inner)), out_...  61.9 us
    unnamed x1, local copies, waits for them, and re-layouts  1.47 us

profile of v3, /device:TPU:0, one launch (start us, length us, event | category | flops | bytes accessed | tf_op | source)
XLA Modules:
  0.0 67.0 jit_solution(16711218101607180265)
XLA Ops:
  1.9 61.9 %shard_map.86 = (f32[1,128,128]{2,1,0:T(8,128)}, f32[1]{0:T(128)}) custom-call(bf16[128,3584]{1,0:T(8,128)(2,1)} %tok_hbm.1, bf16[128,14336]{1,0:T(8,128)(2,1)} %og_hbm.1, bf16[5,128,128]{2,1,0:T(8,128)(2,1)} %bv_hbm.1, s32[2,5]{1,0:T(2,128)} %bitcast.2, s32[1]{0:T(128)S(6)} %copy.11.drops, s32[2,16]{1,0:T(2,128)} %bitcast.3, s32[1]{0:T(128)S(6)} %copy.12.counts), custom_call_target="tpu_custom_call" | custom-call | flops 335544320 | bytes 4587520 | tf_op jit(solution)/shard_map/pallas_call | solution.py:409
  63.8 1.5 %copy.13 = f32[1,128,128]{2,1,0:T(8,128)} copy(f32[1,128,128]{2,1,0:T(8,128)} %get-tuple-element.4) | data formatting | bytes 131072

commit v4 on v2

--- a/solution.py
+++ b/solution.py
@@ -175,34 +175,43 @@
 
     turned = n_cand // (outer * inner)
 
-    @pl.loop(0, 2 * outer - 1)
-    def _(i):
-        a = around(i, my_a)
-
-        @pl.loop(0, 2 * inner - 1)
-        def _(j):
-            b = around(j, my_b)
-
-            @pl.when((a >= 0) & (a < outer) & (b >= 0) & (b < inner))
+    steps = outer * inner
+
+    def nearest(step, mine, size):
+        ends = jnp.minimum(mine, size - 1 - mine)
+        rest = jnp.where(mine < size - 1 - mine, step, size - 1 - step)
+        return jnp.where(step <= 2 * ends, around(step, mine), rest)
+
+    def place_at(step):
+        return nearest(step // inner, my_a, outer), nearest(step % inner, my_b, inner)
+
+    @pl.loop(0, steps + 1)
+    def _(step):
+        @pl.when((step > 0) & (step < steps))
+        def _():
+            a, b = place_at(step)
+            chunk_copy(index(a, b, core), 4, sibling).wait_recv()
+            forwards(a, b, lambda copy: copy.start())
+
+        @pl.loop(0, 2)
+        def _(turn):
+            at = step - 1 + turn
+
+            @pl.when((at >= 0) & (at < steps))
             def _():
-                @pl.when(i + j > 0)
+                a, b = place_at(at)
+
+                @pl.when(turn == 0)
                 def _():
-                    chunk_copy(index(a, b, core), 4, sibling).wait_recv()
-                    forwards(a, b, lambda copy: copy.start())
-
-                for at in range(turned):
-                    c = (a * inner + b) * turned + at
-                    xt[c] = tok[cands[0, c]].T
-
-                @pl.loop(0, 2)
-                def _(turn):
-                    source = index(a, b, (core + turn) % 2)
-
-                    @pl.when(turn == 1)
-                    def _():
-                        chunk_copy(source, 4, sibling).wait_recv()
-
-                    process(source)
+                    chunk_copy(index(a, b, 1 - core), 4, sibling).wait_recv()
+
+                process(index(a, b, (core + 1 + turn) % 2))
+
+        @pl.when(step < steps)
+        def _():
+            for at in range(turned):
+                c = step * turned + at
+                xt[c] = tok[cands[0, c]].T
 
     wait_columns(og, load_sem.at[2])
     position = me * blk + lax.broadcasted_iota(jnp.int32, (blk, 1), 0)
@@ -382,7 +391,7 @@
             sem((outer,)), sem((outer,)), sem((n_dp,)), sem((n_dp,)),
         ],
         compiler_params=pltpu.CompilerParams(
-            collective_id=0, has_side_effects=True, vmem_limit_bytes=64 * 1024 * 1024
+            collective_id=0, has_side_effects=True, vmem_limit_bytes=64 * 1024 * 1024 - 128 * 1024
         ),
         cost_estimate=pl.CostEstimate(
             flops=2 * blk ** 3 * (n_f * kept + n_cand),

time: 57.8 us -> 52.4 us (0.907)
  Pallas kernels: 52.4 us -> 47 us
    pallas_call x1, Pallas kernels: 52.4 us -> 47 us  [per_device(): pl.pallas_call(functools.partial(kernel, (n_dp, n_f, outer, inner)), out_...]
where the time goes in v4:
time: 52.4 us; the launch traced here: 52.1 us
  Pallas kernels  47 us (90%)
  between operations  3.68 us (7%)
  local copies, waits for them, and re-layouts  1.47 us (3%)
    pallas_call x1, Pallas kernels, per_device(): pl.pallas_call(functools.partial(kernel, (n_dp, n_f, outer, inner)), out_...  47 us
    unnamed x1, local copies, waits for them, and re-layouts  1.47 us

profile of v4, /device:TPU:0, one launch (start us, length us, event | category | flops | bytes accessed | tf_op | source)
XLA Modules:
  0.0 52.1 jit_solution(14049224680415553552)
XLA Ops:
  1.9 47.0 %shard_map.86 = (f32[1,128,128]{2,1,0:T(8,128)}, f32[1]{0:T(128)}) custom-call(bf16[128,3584]{1,0:T(8,128)(2,1)} %tok_hbm.1, bf16[128,14336]{1,0:T(8,128)(2,1)} %og_hbm.1, bf16[5,128,128]{2,1,0:T(8,128)(2,1)} %bv_hbm.1, s32[2,5]{1,0:T(2,128)} %bitcast.2, s32[1]{0:T(128)S(6)} %copy.11.drops, s32[2,16]{1,0:T(2,128)} %bitcast.3, s32[1]{0:T(128)S(6)} %copy.12.counts), custom_call_target="tpu_custom_call" | custom-call | flops 335544320 | bytes 4587520 | tf_op jit(solution)/shard_map/pallas_call | solution.py:358
  48.9 1.5 %copy.13 = f32[1,128,128]{2,1,0:T(8,128)} copy(f32[1,128,128]{2,1,0:T(8,128)} %get-tuple-element.4) | data formatting | bytes 131072

commit v5 on v4

--- a/solution.py
+++ b/solution.py
@@ -19,10 +19,10 @@
     dims,
     tok_hbm, og_hbm, bv_hbm, active, drops, cands, counts,
     grad_out, score_out,
-    tok, og, bv, gath, meta_v, meta_s, xt, prod, acc,
-    send_a, recv_a, own_a, send_c, recv_c, own_c, send_d, recv_d, share_b,
+    tok, og, bv, gath, meta_v, meta_s, xt, sums, acc,
+    send_a, recv_a, own_a, send_c, recv_c, own_c, send_d, recv_d,
     load_sem, meta_send, meta_recv, meta_load, chunk_send, chunk_recv,
-    a_send, a_recv, c_send, c_recv, d_send, d_recv, b_send, b_recv,
+    a_send, a_recv, c_send, c_recv, d_send, d_recv,
 ):
     n_dp, n_f, outer, inner = dims
     blk = bv.shape[1]
@@ -61,9 +61,21 @@
 
     @pl.loop(1, n_dp)
     def _(step):
-        pl.semaphore_signal(
-            barrier, inc=1, device_id={"dp": (dp + step) % n_dp}, device_id_type=MESH
-        )
+        def greet(a, b):
+            pl.semaphore_signal(
+                barrier,
+                inc=1,
+                device_id={"dp": (dp + step) % n_dp, "fsdp": index(a, b, core)},
+                device_id_type=MESH,
+            )
+
+        @pl.loop(0, inner)
+        def _(b):
+            greet(my_a, b)
+
+        @pl.loop(1, outer)
+        def _(hop):
+            greet((my_a + hop) % outer, my_b)
 
     load_columns(tok_hbm, tok, load_sem.at[1])
     drop = drops[0]
@@ -77,7 +89,7 @@
         places = jnp.where(lane == 2 * slot + 1, active[1, at], places)
     meta_v[me] = places
 
-    pl.semaphore_wait(barrier, n_f - 1 + n_dp - 1)
+    pl.semaphore_wait(barrier, n_f - 1 + (n_dp - 1) * (inner + outer - 1))
 
     def chunk_copy(source, way, target):
         return pltpu.make_async_remote_copy(
@@ -151,27 +163,32 @@
     to_scalars.start()
     to_scalars.wait()
 
-    def process(source):
+    for turn in range(2):
+        sums[turn, 0] = jnp.zeros(sums.shape[2:], jnp.float32)
+
+    def products(source, turn):
         for slot in range(kept):
-            prod[slot] = jnp.dot(
+            sums[turn, 1 << slot] = jnp.dot(
                 tok[meta_s[source, 0, 2 * slot]],
                 gath[source, slot * blk:(slot + 1) * blk, :],
                 preferred_element_type=jnp.float32,
             )
-        columns = [meta_s[source, 0, 2 * slot + 1] for slot in range(kept)]
-        for top in range(0, blk, 64):
-            part = [prod[slot, top:top + 64, :] for slot in range(kept)]
-
-            @pl.loop(0, n_cand // 16)
-            def _(group):
-                for at in range(16):
-                    c = group * 16 + at
-                    column = cands[1, c]
-                    total = acc[c, top:top + 64, :]
-                    for slot in range(kept):
-                        chosen = jnp.where(columns[slot] == column, 1.0, 0.0)
-                        total = total + chosen * part[slot]
-                    acc[c, top:top + 64, :] = total
+
+        @pl.loop(0, blk // 32)
+        def _(part):
+            rows = pl.ds(pl.multiple_of(part * 32, 32), 32)
+            found = [None] * (1 << kept)
+            for slot in range(kept):
+                found[1 << slot] = sums[turn, 1 << slot, rows, :]
+                for low in range(1, 1 << slot):
+                    found[low + (1 << slot)] = found[low] + found[1 << slot]
+                    sums[turn, low + (1 << slot), rows, :] = found[low + (1 << slot)]
+
+    def chosen(source, column, valid):
+        bits = jnp.int32(0)
+        for slot in range(kept):
+            bits = bits + jnp.where(meta_s[source, 0, 2 * slot + 1] == column, 1 << slot, 0)
+        return bits * valid
 
     turned = n_cand // (outer * inner)
 
@@ -193,19 +210,29 @@
             chunk_copy(index(a, b, core), 4, sibling).wait_recv()
             forwards(a, b, lambda copy: copy.start())
 
-        @pl.loop(0, 2)
-        def _(turn):
-            at = step - 1 + turn
-
-            @pl.when((at >= 0) & (at < steps))
-            def _():
-                a, b = place_at(at)
-
-                @pl.when(turn == 0)
-                def _():
-                    chunk_copy(index(a, b, 1 - core), 4, sibling).wait_recv()
-
-                process(index(a, b, (core + 1 + turn) % 2))
+        before = place_at(jnp.maximum(step - 1, 0))
+        now = place_at(jnp.minimum(step, steps - 1))
+        other, source = index(*before, 1 - core), index(*now, core)
+
+        @pl.when(step > 0)
+        def _():
+            chunk_copy(other, 4, sibling).wait_recv()
+            products(other, 0)
+
+        @pl.when(step < steps)
+        def _():
+            products(source, 1)
+
+        has_other = jnp.where(step > 0, 1, 0)
+        has_own = jnp.where(step < steps, 1, 0)
+
+        @pl.loop(0, n_cand // 4)
+        def _(group):
+            for at in range(4):
+                c = group * 4 + at
+                first = chosen(other, cands[1, c], has_other)
+                second = chosen(source, cands[1, c], has_own)
+                acc[c] = acc[c] + (sums[0, first] + sums[1, second])
 
         @pl.when(step < steps)
         def _():
@@ -230,25 +257,32 @@
             device_id={"fsdp": sibling}, device_id_type=MESH,
         )
 
-    def c_copy(a, step):
-        return pltpu.make_async_remote_copy(
-            src_ref=send_c.at[step, a], dst_ref=recv_c.at[step, a],
-            send_sem=c_send.at[step, a], recv_sem=c_recv.at[step, a],
-            device_id={"fsdp": index(my_a, (my_b + step) % inner, core)}, device_id_type=MESH,
-        )
-
-    def d_copy(step):
-        return pltpu.make_async_remote_copy(
-            src_ref=send_d.at[step], dst_ref=recv_d.at[step],
-            send_sem=d_send.at[step], recv_sem=d_recv.at[step],
-            device_id={"fsdp": index((my_a + step) % outer, my_b, core)}, device_id_type=MESH,
-        )
-
-    def b_copy(step):
-        return pltpu.make_async_remote_copy(
-            src_ref=share_b.at[0], dst_ref=share_b.at[step],
-            send_sem=b_send.at[step], recv_sem=b_recv.at[step],
-            device_id={"dp": (dp + step) % n_dp}, device_id_type=MESH,
+    def c_copy(a, b):
+        return pltpu.make_async_remote_copy(
+            src_ref=send_c.at[b, a], dst_ref=recv_c.at[dp, my_b, a],
+            send_sem=c_send.at[b, a], recv_sem=c_recv.at[dp, my_b, a],
+            device_id={"dp": a % n_dp, "fsdp": index(my_a, b, core)}, device_id_type=MESH,
+        )
+
+    def c_arrival(group, b, a):
+        return pltpu.make_async_remote_copy(
+            src_ref=recv_c.at[group, b, a], dst_ref=recv_c.at[group, b, a],
+            send_sem=c_send.at[b, a], recv_sem=c_recv.at[group, b, a],
+            device_id={"fsdp": sibling}, device_id_type=MESH,
+        )
+
+    def d_copy(a, group):
+        return pltpu.make_async_remote_copy(
+            src_ref=send_d.at[a], dst_ref=recv_d.at[my_a],
+            send_sem=d_send.at[a, group], recv_sem=d_recv.at[my_a],
+            device_id={"dp": group, "fsdp": index(a, my_b, core)}, device_id_type=MESH,
+        )
+
+    def d_arrival(a):
+        return pltpu.make_async_remote_copy(
+            src_ref=recv_d.at[a], dst_ref=recv_d.at[a],
+            send_sem=d_send.at[0, 0], recv_sem=d_recv.at[a],
+            device_id={"fsdp": sibling}, device_id_type=MESH,
         )
 
     def every(act):
@@ -258,9 +292,9 @@
 
             @pl.loop(0, outer // 2)
             def _(pair):
-                act(step, b, [(my_a + 2 * pair + hop) % outer for hop in (1, 2)])
-
-    def for_sibling(step, b, pair):
+                act(b, [(dp + 1 + pair) % 2 + 2 * at for at in range(2)])
+
+    def for_sibling(b, pair):
         found = [term(index(a, b, 1 - core)) for a in pair]
         for a, value in zip(pair, found):
             send_a[a * inner + b] = value.astype(jnp.bfloat16)
@@ -268,7 +302,7 @@
 
     every(for_sibling)
 
-    def for_mine(step, b, pair):
+    def for_mine(b, pair):
         found = [term(index(a, b, core)) for a in pair]
         for at, value in enumerate(found):
             own_a[at] = value
@@ -276,12 +310,14 @@
             a_copy(a, b).wait_recv()
             total = own_a[at] + recv_a[a * inner + b].astype(jnp.float32)
 
-            @pl.when(step < inner)
+            here = (b == my_b) & (a % n_dp == dp)
+
+            @pl.when(jnp.logical_not(here))
             def _():
-                send_c[step, a] = total.astype(jnp.bfloat16)
-                c_copy(a, step).start()
-
-            @pl.when(step == inner)
+                send_c[b, a] = total.astype(jnp.bfloat16)
+                c_copy(a, b).start()
+
+            @pl.when(here)
             def _():
                 own_c[a] = total
 
@@ -290,32 +326,41 @@
     @pl.loop(1, outer + 1)
     def _(hop):
         a = (my_a + hop) % outer
-        total = own_c[a]
-        for step in range(1, inner):
-            c_copy(a, step).wait_recv()
-            total = total + recv_c[step, a].astype(jnp.float32)
-
-        @pl.when(hop < outer)
-        def _():
-            send_d[hop] = total.astype(jnp.bfloat16)
-            d_copy(hop).start()
-
-        @pl.when(hop == outer)
-        def _():
-            own_c[a] = total
-
-    total = own_c[my_a]
-    for hop in range(1, outer):
-        d_copy(hop).wait_recv()
-        total = total + recv_d[hop].astype(jnp.float32)
-    share_b[0] = total.astype(jnp.bfloat16)
-    for step in range(1, n_dp):
-        b_copy(step).start()
-    for step in range(1, n_dp):
-        b_copy(step).wait_recv()
-    total = jnp.zeros((blk, blk), jnp.float32)
-    for group in range(n_dp):
-        total = total + share_b[(dp - group + n_dp) % n_dp].astype(jnp.float32)
+
+        @pl.when(a % n_dp == dp)
+        def _():
+            @pl.loop(1, n_dp * inner)
+            def _(step):
+                group = (dp + step // inner) % n_dp
+                b = (my_b + step % inner) % inner
+                c_arrival(group, b, a).wait_recv()
+                own_c[a] = own_c[a] + recv_c[group, b, a].astype(jnp.float32)
+
+            send_d[a] = own_c[a].astype(jnp.bfloat16)
+
+            @pl.loop(1, n_dp + 1)
+            def _(step):
+                group = (dp + step) % n_dp
+
+                @pl.when((group != dp) | (a != my_a))
+                def _():
+                    d_copy(a, group).start()
+
+            @pl.when(a == my_a)
+            def _():
+                recv_d[my_a] = send_d[a]
+
+    own_a[0] = jnp.zeros((blk, blk), jnp.float32)
+
+    @pl.loop(0, outer)
+    def _(a):
+        @pl.when((a != my_a) | (my_a % n_dp != dp))
+        def _():
+            d_arrival(a).wait_recv()
+
+        own_a[0] = own_a[0] + recv_d[a].astype(jnp.float32)
+
+    total = own_a[0]
     scale = (blk * n_dp * n_f) ** (-0.5)
     total = total * scale
     grad_out[0] = total
@@ -333,13 +378,17 @@
             forwards(a, b, lambda copy: copy.wait_send())
             a_copy(a, b).wait_send()
 
-        for step in range(1, inner):
-            c_copy(a, step).wait_send()
-
-    for hop in range(1, outer):
-        d_copy(hop).wait_send()
-    for step in range(1, n_dp):
-        b_copy(step).wait_send()
+            @pl.when((b != my_b) | (a % n_dp != dp))
+            def _():
+                c_copy(a, b).wait_send()
+
+        @pl.when(a % n_dp == dp)
+        def _():
+            @pl.loop(0, n_dp)
+            def _(group):
+                @pl.when((group != dp) | (a != my_a))
+                def _():
+                    d_copy(a, group).wait_send()
 
 
 def per_device(
@@ -375,20 +424,19 @@
             pltpu.VMEM((n_f, 1, 128), i32),
             pltpu.SMEM((n_f, 1, 128), i32),
             pltpu.VMEM((n_cand, blk, rows), bf16),
-            pltpu.VMEM((kept, rows, blk), f32),
+            pltpu.VMEM((2, 1 << kept, rows, blk), f32),
             pltpu.VMEM((n_cand, rows, blk), f32),
             pltpu.VMEM((half, blk, blk), bf16),
             pltpu.VMEM((half, blk, blk), bf16),
             pltpu.VMEM((2, blk, blk), f32),
             pltpu.VMEM((inner, outer, blk, blk), bf16),
-            pltpu.VMEM((inner, outer, blk, blk), bf16),
+            pltpu.VMEM((n_dp, inner, outer, blk, blk), bf16),
             pltpu.VMEM((outer, blk, blk), f32),
             pltpu.VMEM((outer, blk, blk), bf16),
             pltpu.VMEM((outer, blk, blk), bf16),
-            pltpu.VMEM((n_dp, blk, blk), bf16),
             sem((3,)), sem((n_f,)), sem((n_f,)), sem(()), sem((5, n_f)), sem((n_f,)),
-            sem((half,)), sem((half,)), sem((inner, outer)), sem((inner, outer)),
-            sem((outer,)), sem((outer,)), sem((n_dp,)), sem((n_dp,)),
+            sem((half,)), sem((half,)), sem((inner, outer)), sem((n_dp, inner, outer)),
+            sem((outer, n_dp)), sem((outer,)),
         ],
         compiler_params=pltpu.CompilerParams(
             collective_id=0, has_side_effects=True, vmem_limit_bytes=64 * 1024 * 1024 - 128 * 1024

time: 52.4 us -> 52.4 us (level)
  no operation moved by 1% of the time
where the time goes in v5:
time: 52.4 us; the launch traced here: 52.1 us
  Pallas kernels  47 us (90%)
  between operations  3.68 us (7%)
  local copies, waits for them, and re-layouts  1.47 us (3%)
    pallas_call x1, Pallas kernels, per_device(): pl.pallas_call(functools.partial(kernel, (n_dp, n_f, outer, inner)), out_...  47 us
    unnamed x1, local copies, waits for them, and re-layouts  1.47 us

profile of v5, /device:TPU:0, one launch (start us, length us, event | category | flops | bytes accessed | tf_op | source)
XLA Modules:
  0.0 52.1 jit_solution(6289316483355401705)
XLA Ops:
  1.9 47.0 %shard_map.86 = (f32[1,128,128]{2,1,0:T(8,128)}, f32[1]{0:T(128)}) custom-call(bf16[128,3584]{1,0:T(8,128)(2,1)} %tok_hbm.1, bf16[128,14336]{1,0:T(8,128)(2,1)} %og_hbm.1, bf16[5,128,128]{2,1,0:T(8,128)(2,1)} %bv_hbm.1, s32[2,5]{1,0:T(2,128)} %bitcast.2, s32[1]{0:T(128)S(6)} %copy.11.drops, s32[2,16]{1,0:T(2,128)} %bitcast.3, s32[1]{0:T(128)S(6)} %copy.12.counts), custom_call_target="tpu_custom_call" | custom-call | flops 335544320 | bytes 4587520 | tf_op jit(solution)/shard_map/pallas_call | solution.py:407
  48.9 1.5 %copy.13 = f32[1,128,128]{2,1,0:T(8,128)} copy(f32[1,128,128]{2,1,0:T(8,128)} %get-tuple-element.4) | data formatting | bytes 131072

commit v6 on v5

--- a/solution.py
+++ b/solution.py
@@ -28,6 +28,7 @@
     blk = bv.shape[1]
     stored = bv.shape[0]
     kept = stored - 1
+    split = kept // 2
     n_cand = acc.shape[0]
     dp = lax.axis_index("dp")
     me = lax.axis_index("fsdp")
@@ -84,19 +85,19 @@
     load_bv.wait()
     for slot in range(kept):
         at = slot + jnp.where(drop <= slot, 1, 0)
-        gath[me, slot * blk:(slot + 1) * blk, :] = bv[at]
+        gath[me, slot // split, slot % split * blk:(slot % split + 1) * blk, :] = bv[at]
         places = jnp.where(lane == 2 * slot, active[0, at], places)
         places = jnp.where(lane == 2 * slot + 1, active[1, at], places)
     meta_v[me] = places
 
     pl.semaphore_wait(barrier, n_f - 1 + (n_dp - 1) * (inner + outer - 1))
 
-    def chunk_copy(source, way, target):
-        return pltpu.make_async_remote_copy(
-            src_ref=gath.at[source],
-            dst_ref=gath.at[source],
-            send_sem=chunk_send.at[way, source],
-            recv_sem=chunk_recv.at[source],
+    def chunk_copy(source, half, way, target):
+        return pltpu.make_async_remote_copy(
+            src_ref=gath.at[source, half],
+            dst_ref=gath.at[source, half],
+            send_sem=chunk_send.at[way, source, half],
+            recv_sem=chunk_recv.at[source, half],
             device_id={"fsdp": target},
             device_id_type=MESH,
         )
@@ -122,26 +123,26 @@
             device_id_type=MESH,
         )
 
-    def forwards(a, b, act):
+    def forwards(a, b, half, act):
         source = index(a, b, core)
 
         @pl.when((b == my_b) & (a >= my_a) & (my_a > 0))
         def _():
-            act(chunk_copy(source, 0, index(my_a - 1, my_b, core)))
+            act(chunk_copy(source, half, 0, index(my_a - 1, my_b, core)))
 
         @pl.when((b == my_b) & (a <= my_a) & (my_a < outer - 1))
         def _():
-            act(chunk_copy(source, 1, index(my_a + 1, my_b, core)))
+            act(chunk_copy(source, half, 1, index(my_a + 1, my_b, core)))
 
         @pl.when((b >= my_b) & (my_b > 0))
         def _():
-            act(chunk_copy(source, 2, index(my_a, my_b - 1, core)))
+            act(chunk_copy(source, half, 2, index(my_a, my_b - 1, core)))
 
         @pl.when((b <= my_b) & (my_b < inner - 1))
         def _():
-            act(chunk_copy(source, 3, index(my_a, my_b + 1, core)))
-
-        act(chunk_copy(source, 4, sibling))
+            act(chunk_copy(source, half, 3, index(my_a, my_b + 1, core)))
+
+        act(chunk_copy(source, half, 4, sibling))
 
     def around(step, mine):
         return mine + (1 - 2 * (step % 2)) * ((step + 1) // 2)
@@ -150,7 +151,8 @@
     def _(step):
         meta_copy(step).start()
 
-    forwards(my_a, my_b, lambda copy: copy.start())
+    for half in range(2):
+        forwards(my_a, my_b, half, lambda copy: copy.start())
     load_columns(og_hbm, og, load_sem.at[2])
     wait_columns(tok, load_sem.at[1])
     acc[...] = jnp.zeros(acc.shape, jnp.float32)
@@ -170,7 +172,7 @@
         for slot in range(kept):
             sums[turn, 1 << slot] = jnp.dot(
                 tok[meta_s[source, 0, 2 * slot]],
-                gath[source, slot * blk:(slot + 1) * blk, :],
+                gath[source, slot // split, slot % split * blk:(slot % split + 1) * blk, :],
                 preferred_element_type=jnp.float32,
             )
 
@@ -207,8 +209,11 @@
         @pl.when((step > 0) & (step < steps))
         def _():
             a, b = place_at(step)
-            chunk_copy(index(a, b, core), 4, sibling).wait_recv()
-            forwards(a, b, lambda copy: copy.start())
+
+            @pl.loop(0, 2)
+            def _(half):
+                chunk_copy(index(a, b, core), half, 4, sibling).wait_recv()
+                forwards(a, b, half, lambda copy: copy.start())
 
         before = place_at(jnp.maximum(step - 1, 0))
         now = place_at(jnp.minimum(step, steps - 1))
@@ -216,7 +221,8 @@
 
         @pl.when(step > 0)
         def _():
-            chunk_copy(other, 4, sibling).wait_recv()
+            for half in range(2):
+                chunk_copy(other, half, 4, sibling).wait_recv()
             products(other, 0)
 
         @pl.when(step < steps)
@@ -323,6 +329,16 @@
 
     every(for_mine)
 
+    @pl.loop(1, n_f)
+    def _(step):
+        meta_copy(step).wait_send()
+
+    @pl.loop(0, steps)
+    def _(step):
+        a, b = step // inner, step % inner
+        for half in range(2):
+            forwards(a, b, half, lambda copy: copy.wait_send())
+
     @pl.loop(1, outer + 1)
     def _(hop):
         a = (my_a + hop) % outer
@@ -350,6 +366,15 @@
             def _():
                 recv_d[my_a] = send_d[a]
 
+    @pl.loop(0, steps)
+    def _(step):
+        a, b = step // inner, step % inner
+        a_copy(a, b).wait_send()
+
+        @pl.when((b != my_b) | (a % n_dp != dp))
+        def _():
+            c_copy(a, b).wait_send()
+
     own_a[0] = jnp.zeros((blk, blk), jnp.float32)
 
     @pl.loop(0, outer)
@@ -367,21 +392,8 @@
     score = jnp.sqrt(jnp.sum(total * total, keepdims=True) * (1.0 / (blk * blk)) + 1e-06)
     score_out[0] = score[0, 0]
 
-    @pl.loop(1, n_f)
-    def _(step):
-        meta_copy(step).wait_send()
-
     @pl.loop(0, outer)
     def _(a):
-        @pl.loop(0, inner)
-        def _(b):
-            forwards(a, b, lambda copy: copy.wait_send())
-            a_copy(a, b).wait_send()
-
-            @pl.when((b != my_b) | (a % n_dp != dp))
-            def _():
-                c_copy(a, b).wait_send()
-
         @pl.when(a % n_dp == dp)
         def _():
             @pl.loop(0, n_dp)
@@ -420,7 +432,7 @@
             pltpu.VMEM((tokens.shape[1] // blk, rows, blk), bf16),
             pltpu.VMEM((out_grad.shape[1] // blk, rows, blk), bf16),
             pltpu.VMEM(block_values.shape, bf16),
-            pltpu.VMEM((n_f, kept * blk, blk), bf16),
+            pltpu.VMEM((n_f, 2, kept // 2 * blk, blk), bf16),
             pltpu.VMEM((n_f, 1, 128), i32),
             pltpu.SMEM((n_f, 1, 128), i32),
             pltpu.VMEM((n_cand, blk, rows), bf16),
@@ -434,7 +446,7 @@
             pltpu.VMEM((outer, blk, blk), f32),
             pltpu.VMEM((outer, blk, blk), bf16),
             pltpu.VMEM((outer, blk, blk), bf16),
-            sem((3,)), sem((n_f,)), sem((n_f,)), sem(()), sem((5, n_f)), sem((n_f,)),
+            sem((3,)), sem((n_f,)), sem((n_f,)), sem(()), sem((5, n_f, 2)), sem((n_f, 2)),
             sem((half,)), sem((half,)), sem((inner, outer)), sem((n_dp, inner, outer)),
             sem((outer, n_dp)), sem((outer,)),
         ],

time: 52.4 us -> 52 us (level)
  no operation moved by 1% of the time
where the time goes in v6:
time: 52 us; the launch traced here: 51.8 us
  Pallas kernels  46.6 us (90%)
  between operations  3.68 us (7%)
  local copies, waits for them, and re-layouts  1.47 us (3%)
    pallas_call x1, Pallas kernels, per_device(): pl.pallas_call(functools.partial(kernel, (n_dp, n_f, outer, inner)), out_...  46.6 us
    unnamed x1, local copies, waits for them, and re-layouts  1.47 us

profile of v6, /device:TPU:0, one launch (start us, length us, event | category | flops | bytes accessed | tf_op | source)
XLA Modules:
  0.0 51.8 jit_solution(11758180751318712983)
XLA Ops:
  1.9 46.6 %shard_map.86 = (f32[1,128,128]{2,1,0:T(8,128)}, f32[1]{0:T(128)}) custom-call(bf16[128,3584]{1,0:T(8,128)(2,1)} %tok_hbm.1, bf16[128,14336]{1,0:T(8,128)(2,1)} %og_hbm.1, bf16[5,128,128]{2,1,0:T(8,128)(2,1)} %bv_hbm.1, s32[2,5]{1,0:T(2,128)} %bitcast.2, s32[1]{0:T(128)S(6)} %copy.11.drops, s32[2,16]{1,0:T(2,128)} %bitcast.3, s32[1]{0:T(128)S(6)} %copy.12.counts), custom_call_target="tpu_custom_call" | custom-call | flops 335544320 | bytes 4587520 | tf_op jit(solution)/shard_map/pallas_call | solution.py:419
  48.6 1.5 %copy.13 = f32[1,128,128]{2,1,0:T(8,128)} copy(f32[1,128,128]{2,1,0:T(8,128)} %get-tuple-element.4) | data formatting | bytes 131072
